TPU v7x, 32 devices: a whole 2x2x4 slice. The times are simulated.
32 devices in a mesh: group: 4 (over y, core), blk: 8 (over z, x).
Axes of the slice: x: 2, y: 2, z: 4, core: 2. Of those that a mesh axis runs over, the one named last changes fastest.
Arguments:
- queries: bfloat16 [2048, 32, 128], P('blk'), may hold values from -8 to 8
- doc_blocks: bfloat16 [4, 128, 128, 128], P('group', 'blk'), may hold values from -2 to 2
- doc_len: int32 [4, 128], P('group', 'blk'), may hold values from 96 to 128
- candidates: int32 [4, 8, 4, 8], P('group', 'blk'), may hold values from 0 to 17, as said below
- cand_count: int32 [4, 8, 4], P('group', 'blk'), may hold values from 2 to 8, as said below
- hot_owned: int32 [4, 8, 1], P('group', 'blk'), may hold values from 0 to 15
- hot_taken: int32 [4, 8, 2], P('group', 'blk'), may hold values from 0 to 7, as said below
Outputs:
- top_scores: float32 [2048, 16], P('blk')
Inputs may be any that keep to these rules, and one draw needn't show every extreme that they name: `candidates`: slots below 16 name a device's own blocks, the others its hot copies; entries at or past the hop's count are ignored. `cand_count`: every query block has 8 live candidates at one or more of its hops. `hot_taken`: entries are hot pool indices of the same group; every pool entry is held by some device.
All inputs are finite; a program needn't handle non-finite values.
Results may differ from a plain program's by a relative error of at most 0.0003.
Values may be sent and summed in bfloat16 or wider, within the bound.
A program may use at most 64 MiB of HBM per device.

v0:
```python
import jax
import jax.numpy as jnp
from jax import lax
from jax.sharding import PartitionSpec as P

QTOK = 32
TOPK = 16


MASKED_SCORE = -1e30


def shifted(x, axis, by):
    peers = lax.axis_size(axis)
    return lax.ppermute(x, axis, [(i, (i + by) % peers) for i in range(peers)])


def maxsim(query_part, blocks, lengths):

    def single(element):
        doc_block, length = element
        scores = lax.dot_general(
            query_part, doc_block, (((1,), (1,)), ((), ())), preferred_element_type=jnp.float32
        )
        keep_mask = jnp.arange(doc_block.shape[0], dtype=jnp.int32) < length
        scores = jnp.where(keep_mask[None, :], scores, MASKED_SCORE)
        best_rows = jnp.max(scores, axis=1).reshape(-1, QTOK)
        return jnp.sum(best_rows, axis=1) / QTOK

    return lax.map(single, (blocks, lengths)).T


def masked_scores(query_part, chosen, chosen_len, live_count):
    scores = maxsim(query_part, chosen, chosen_len)
    keep_mask = jnp.arange(chosen.shape[0], dtype=jnp.int32) < live_count
    return jnp.where(keep_mask[None, :], scores, MASKED_SCORE)


def hop_scores(query_part, blocks, lengths, slots, live_count):
    chosen = jnp.take(blocks, slots, axis=0)
    chosen_len = jnp.take(lengths, slots, axis=0)
    return masked_scores(query_part, chosen, chosen_len, live_count)


def on_device(queries, doc_blocks, doc_len, candidates, cand_count, hot_owned, hot_taken):
    lengths_all, cand_all, count_all, taken_all, owned_all = (
        lax.all_gather(doc_len, "blk", axis=1, tiled=True),
        lax.all_gather(candidates, "blk", axis=1, tiled=True),
        lax.all_gather(cand_count, "blk", axis=1, tiled=True),
        lax.all_gather(hot_taken, "blk", axis=1, tiled=True),
        lax.all_gather(hot_owned, "blk", axis=1, tiled=True),
    )
    shards = lax.axis_size("blk")
    position = lax.axis_index("blk")
    per_dev = doc_blocks.shape[1]
    hot_pub = hot_owned.shape[2]
    hot_dev = hot_taken.shape[2]
    hop_total = candidates.shape[2]
    owner_dev = taken_all[0] // hot_pub
    member = taken_all[0] % hot_pub
    hot_ids = owner_dev * per_dev + owned_all[0][owner_dev, member]
    own_ids = (
        jnp.arange(shards, dtype=jnp.int32)[:, None] * per_dev
        + jnp.arange(per_dev, dtype=jnp.int32)[None, :]
    )
    ext_len_all = jnp.take(lengths_all[0], jnp.concatenate([own_ids, hot_ids], axis=1), axis=0)
    local_blocks = doc_blocks[0]
    published = jnp.take(local_blocks, hot_owned[0, 0], axis=0)
    taken_here = hot_taken[0, 0]
    empty_blocks = jnp.zeros((hot_dev,) + local_blocks.shape[1:], local_blocks.dtype)
    shard_piece = lax.all_gather(published, "blk", axis=0, tiled=True)
    row_count = shard_piece.shape[0]
    inside = (taken_here >= 0) & (taken_here < row_count)
    picked = jnp.take(shard_piece, jnp.clip(taken_here, 0, row_count - 1), axis=0)
    hot_blocks = jnp.where(inside[:, None, None], picked, empty_blocks)
    ext_blocks = jnp.concatenate([local_blocks, hot_blocks], axis=0)
    query_rows = queries.reshape(-1, queries.shape[2])
    score_parts = []
    visiting = query_rows
    for hop_number in range(hop_total):
        if hop_number > 0:
            visiting = shifted(visiting, "blk", 1)
        home_dev = (position - hop_number) % shards
        scores = hop_scores(
            visiting,
            ext_blocks,
            ext_len_all[position],
            cand_all[0, home_dev, hop_number],
            count_all[0, home_dev, hop_number],
        )
        if hop_number > 0:
            scores = shifted(scores, "blk", -hop_number)
        score_parts.append(scores)
    combined = jnp.concatenate(score_parts, axis=1)
    every_group = lax.all_gather(combined, "group", axis=1, tiled=True)
    top_values = lax.top_k(every_group, TOPK)[0]
    return top_values


def solution(mesh):
    return jax.shard_map(
        on_device,
        mesh=mesh,
        in_specs=(
            P("blk", None, None),
            P("group", "blk", None, None),
            P("group", "blk"),
            P("group", "blk", None, None),
            P("group", "blk", None),
            P("group", "blk", None),
            P("group", "blk", None),
        ),
        out_specs=P("blk", None),
        check_vma=False,
    )
```

profile of v0, /device:TPU:27, one launch (start us, length us, event | category | flops | bytes accessed | tf_op | source)
XLA Modules:
  0.0 284.3 jit_solution(9362428100582840750)
XLA Ops:
  2.7 51.4 %all_gather.22 = s32[1,8,2]{2,0,1:T(1,128)S(1)} all-gather(s32[1,1,2]{2,0,1:T(1,128)} %bitcast.138), channel_id=1, replica_groups=mesh['group'=4,'blk'=8] {'blk'}, dimensions={1}, use_global_device_ids=true | all-gather | bytes 72 | tf_op jit(solution)/shard_map/all_gather | solution.py:50
  57.7 8.4 %all-reduce.3 = (s32[128]{0:T(128)S(1)}, s32[8]{0:T(128)S(1)}) all-reduce(s32[128]{0:T(128)S(1)} %bitcast_dynamic-update-slice_fusion, s32[8]{0:T(128)S(1)} %bitcast_dynamic-update-slice_fusion.1), channel_id=1, replica_groups=mesh['group'=4,'blk'=8] {'blk'}, use_global_device_ids=true, to_apply=%add.2 | all-reduce | flops 136 | bytes 1088 | tf_op jit(solution)/shard_map/squeeze | solution.py:66
  67.3 1.6 gather_fusion.1
  69.0 20.6 %all_gather.25 = s32[1,8,4,8]{3,2,0,1:T(4,128)S(1)} all-gather(s32[1,1,4,8]{3,2,0,1:T(4,128)S(1)} %bitcast.137), channel_id=1, replica_groups=mesh['group'=4,'blk'=8] {'blk'}, dimensions={1}, use_global_device_ids=true | all-gather | bytes 1152 | tf_op jit(solution)/shard_map/all_gather | solution.py:48
  90.4 24.6 %all-gather = bf16[8,1,128,128]{3,2,1,0:T(8,128)(2,1)S(1)} all-gather(bf16[1,1,128,128]{3,2,1,0:T(8,128)(2,1)S(1)} %dynamic-slice_select_fusion), channel_id=2, replica_groups=mesh['group'=4,'blk'=8] {'blk'}, dimensions={0}, use_global_device_ids=true | all-gather | bytes 294912 | tf_op jit(solution)/shard_map/all_gather | solution.py:71
  116.5 18.0 %while.41 = (s32[]{:T(128)}, f32[8,256]{1,0:T(8,128)S(1)}, s32[8]{0:T(128)S(1)}, bf16[8,128,128]{2,1,0:T(8,128)(2,1)S(1)}, bf16[8192,128]{1,0:T(8,128)(2,1)S(1)}, /*index=5*/s32[]{:T(128)}, f32[]{:T(128)}, s32[]{:T(128)}) while((s32[]{:T(128)}, f32[8,256]{1,0:T(8,128)S(1)}, s32[8]{0:T(128)S(1)}, bf16[8,128,128]{2,1,0:T(8,128)(2,1)S(1)}, ...), condition=%wide.region_3.6_spmd, body=%wide.region_0.5_spmd.sunk | while | flops 270532736 | bytes 2266873 | solution.py:30
  138.3 12.5 %all_gather.21 = s32[1,8,4]{2,0,1:T(1,128)S(1)} all-gather(s32[1,1,4]{2,0,1:T(1,128)S(1)} %bitcast.139), channel_id=1, replica_groups=mesh['group'=4,'blk'=8] {'blk'}, dimensions={1}, use_global_device_ids=true | all-gather | bytes 144 | tf_op jit(solution)/shard_map/all_gather | solution.py:49
  154.1 4.4 %collective-permute-start.2 = (bf16[8192,128]{1,0:T(8,128)(2,1)}, bf16[8192,128]{1,0:T(8,128)(2,1)}, u32[]{:S(2)}, u32[]{:S(2)}) collective-permute-start(bf16[8192,128]{1,0:T(8,128)(2,1)} %collective-permute-done), channel_id=1, source_target_pairs={{0,1},{1,2},{2,3},{3,4},{4,5},{5,6},{6,7},{7,0},{8,9},{9,10},{10,1... | collective-permute-start | bytes 6291464 | tf_op jit(solution)/shard_map/ppermute | solution.py:15
  158.5 31.7 %while.42 = (s32[]{:T(128)}, f32[8,256]{1,0:T(8,128)S(1)}, s32[8]{0:T(128)S(1)}, bf16[8,128,128]{2,1,0:T(8,128)(2,1)S(1)}, bf16[8192,128]{1,0:T(8,128)(2,1)}, /*index=5*/s32[]{:T(128)}, f32[]{:T(128)}, s32[]{:T(128)}) while((s32[]{:T(128)}, f32[8,256]{1,0:T(8,128)S(1)}, s32[8]{0:T(128)S(1)}, bf16[8,128,128]{2,1,0:T(8,128)(2,1)S(1)}, ...), condition=%wide.region_7.10_spmd, body=%wide.region_4.9_spmd.sunk | while | flops 270532736 | bytes 2266873 | solution.py:30
  159.9 2.3 fusion.46
  163.9 2.3 fusion.46
  167.8 2.3 fusion.46
  171.8 2.3 fusion.46
  175.8 2.3 fusion.46
  179.7 2.3 fusion.46
  183.7 2.3 fusion.46
  187.7 2.3 fusion.46
  190.4 4.1 %collective-permute-start.4 = (bf16[8192,128]{1,0:T(8,128)(2,1)}, bf16[8192,128]{1,0:T(8,128)(2,1)S(1)}, u32[]{:S(2)}, u32[]{:S(2)}) collective-permute-start(bf16[8192,128]{1,0:T(8,128)(2,1)} %collective-permute-done.2), channel_id=1, source_target_pairs={{0,1},{1,2},{2,3},{3,4},{4,5},{5,6},{6,7},{7,0},{8,9},{9,10},{10,1... | collective-permute-start | bytes 6291464 | tf_op jit(solution)/shard_map/ppermute | solution.py:15
  194.5 31.7 %while.43 = (s32[]{:T(128)}, f32[8,256]{1,0:T(8,128)S(1)}, s32[8]{0:T(128)S(1)}, bf16[8,128,128]{2,1,0:T(8,128)(2,1)S(1)}, bf16[8192,128]{1,0:T(8,128)(2,1)}, /*index=5*/s32[]{:T(128)}, f32[]{:T(128)}, s32[]{:T(128)}) while((s32[]{:T(128)}, f32[8,256]{1,0:T(8,128)S(1)}, s32[8]{0:T(128)S(1)}, bf16[8,128,128]{2,1,0:T(8,128)(2,1)S(1)}, ...), condition=%wide.region_11.14_spmd, body=%wide.region_8.13_spmd.sunk | while | flops 270532736 | bytes 2266873 | solution.py:30
  195.9 2.3 fusion.49
  199.8 2.3 fusion.49
  203.8 2.3 fusion.49
  207.8 2.3 fusion.49
  211.7 2.3 fusion.49
  215.7 2.3 fusion.49
  219.7 2.3 fusion.49
  223.6 2.3 fusion.49
  226.3 7.4 %collective-permute-done.4 = bf16[8192,128]{1,0:T(8,128)(2,1)S(1)} collective-permute-done((bf16[8192,128]{1,0:T(8,128)(2,1)}, bf16[8192,128]{1,0:T(8,128)(2,1)S(1)}, u32[]{:S(2)}, u32[]{:S(2)}) %collective-permute-start.4) | collective-permute-done | bytes 2097184 | tf_op jit(solution)/shard_map/ppermute | solution.py:15
  233.7 18.9 %while.44 = (s32[]{:T(128)}, f32[8,256]{1,0:T(8,128)S(1)}, s32[8]{0:T(128)S(1)}, bf16[8,128,128]{2,1,0:T(8,128)(2,1)S(1)}, bf16[8192,128]{1,0:T(8,128)(2,1)S(1)}, /*index=5*/s32[]{:T(128)}, f32[]{:T(128)}, s32[]{:T(128)}) while((s32[]{:T(128)}, f32[8,256]{1,0:T(8,128)S(1)}, s32[8]{0:T(128)S(1)}, bf16[8,128,128]{2,1,0:T(8,128)(2,1)S(1)}, ...), condition=%wide.region_15.18_spmd, body=%wide.region_12.17_spmd.sunk | while | flops 270532736 | bytes 2266873 | solution.py:30
  252.8 4.2 %collective-permute-done.5 = f32[256,8]{0,1:T(8,128)S(1)} collective-permute-done((f32[256,8]{0,1:T(8,128)S(1)}, f32[256,8]{0,1:T(8,128)S(1)}, u32[]{:S(2)}, u32[]{:S(2)}) %collective-permute-start.5) | collective-permute-done | bytes 8224 | tf_op jit(solution)/shard_map/ppermute | solution.py:15
  257.0 23.5 %all_gather.27 = f32[256,128]{0,1:T(8,128)S(1)} all-gather(f32[256,32]{0,1:T(8,128)S(1)} %pad_maximum_fusion.1), channel_id=1, replica_groups=mesh['group'=4,'blk'=8] {'group'}, dimensions={1}, use_global_device_ids=true | all-gather | bytes 163840 | tf_op jit(solution)/shard_map/all_gather | solution.py:95
  280.5 3.0 %top_k.9 = (f32[256,128]{0,1:T(8,128)S(1)}, s32[256,128]{0,1:T(8,128)}) sort(f32[256,128]{0,1:T(8,128)S(1)} %all_gather.27, s32[256,128]{0,1:T(8,128)S(1)} %iota.59.clone), dimensions={1}, to_apply=%region_16.19 | sort | flops 491520 | bytes 524288 | tf_op jit(solution)/shard_map/top_k | solution.py:96
  (291 shorter events, 78.1 us)
Async XLA Ops:
  0.0 154.1 %collective-permute-start = (bf16[8192,128]{1,0:T(8,128)(2,1)}, bf16[8192,128]{1,0:T(8,128)(2,1)}, u32[]{:S(2)}, u32[]{:S(2)}) collective-permute-start(bf16[8192,128]{1,0:T(8,128)(2,1)} %bitcast.140), channel_id=1, source_target_pairs={{0,1},{1,2},{2,3},{3,4},{4,5},{5,6},{6,7},{7,0},{8,9},{9,10},{10,1... | collective-permute-start | bytes 6291464 | tf_op jit(solution)/shard_map/ppermute | solution.py:15
  67.3 1.7 copy-start.1
  67.3 23.1 %copy-start = (bf16[1,16,128,128]{3,2,1,0:T(8,128)(2,1)S(1)}, bf16[1,16,128,128]{3,2,1,0:T(8,128)(2,1)}, u32[]{:S(2)}) copy-start(bf16[1,16,128,128]{3,2,1,0:T(8,128)(2,1)} %param.20) | copy-start | bytes 1572868
  68.9 47.6 %copy-start.3 = (bf16[256,32,128]{2,1,0:T(8,128)(2,1)S(1)}, bf16[256,32,128]{2,1,0:T(8,128)(2,1)}, u32[]{:S(2)}) copy-start(bf16[256,32,128]{2,1,0:T(8,128)(2,1)} %param.19) | copy-start | bytes 6291460
  134.5 3.8 %copy-start.2 = (s32[1,1,4]{2,1,0:T(1,128)S(1)}, s32[1,1,4]{2,1,0:T(1,128)}, u32[]{:S(2)}) copy-start(s32[1,1,4]{2,1,0:T(1,128)} %param.23) | copy-start | bytes 52
  154.1 36.2 %collective-permute-start.2 = (bf16[8192,128]{1,0:T(8,128)(2,1)}, bf16[8192,128]{1,0:T(8,128)(2,1)}, u32[]{:S(2)}, u32[]{:S(2)}) collective-permute-start(bf16[8192,128]{1,0:T(8,128)(2,1)} %collective-permute-done), channel_id=1, source_target_pairs={{0,1},{1,2},{2,3},{3,4},{4,5},{5,6},{6,7},{7,0},{8,9},{9,10},{10,1... | collective-permute-start | bytes 6291464 | tf_op jit(solution)/shard_map/ppermute | solution.py:15
  190.3 62.4 %collective-permute-start.1 = (f32[256,8]{0,1:T(8,128)S(1)}, f32[256,8]{0,1:T(8,128)S(1)}, u32[]{:S(2)}, u32[]{:S(2)}) collective-permute-start(f32[256,8]{0,1:T(8,128)S(1)} %select_bitcast_fusion.2), channel_id=1, source_target_pairs={{0,7},{1,0},{2,1},{3,2},{4,3},{5,4},{6,5},{7,6},{8,15},{9,8},{10,9... | collective-permute-start | bytes 24584 | tf_op jit(solution)/shard_map/ppermute | solution.py:15
  190.4 43.3 %collective-permute-start.4 = (bf16[8192,128]{1,0:T(8,128)(2,1)}, bf16[8192,128]{1,0:T(8,128)(2,1)S(1)}, u32[]{:S(2)}, u32[]{:S(2)}) collective-permute-start(bf16[8192,128]{1,0:T(8,128)(2,1)} %collective-permute-done.2), channel_id=1, source_target_pairs={{0,1},{1,2},{2,3},{3,4},{4,5},{5,6},{6,7},{7,0},{8,9},{9,10},{10,1... | collective-permute-start | bytes 6291464 | tf_op jit(solution)/shard_map/ppermute | solution.py:15
  226.3 26.5 %collective-permute-start.3 = (f32[256,8]{0,1:T(8,128)S(1)}, f32[256,8]{0,1:T(8,128)S(1)}, u32[]{:S(2)}, u32[]{:S(2)}) collective-permute-start(f32[256,8]{0,1:T(8,128)S(1)} %select_bitcast_fusion.1), channel_id=1, source_target_pairs={{0,6},{1,7},{2,0},{3,1},{4,2},{5,3},{6,4},{7,5},{8,14},{9,15},{10,... | collective-permute-start | bytes 24584 | tf_op jit(solution)/shard_map/ppermute | solution.py:15
  252.7 4.3 %collective-permute-start.5 = (f32[256,8]{0,1:T(8,128)S(1)}, f32[256,8]{0,1:T(8,128)S(1)}, u32[]{:S(2)}, u32[]{:S(2)}) collective-permute-start(f32[256,8]{0,1:T(8,128)S(1)} %select_bitcast_fusion), channel_id=1, source_target_pairs={{0,5},{1,6},{2,7},{3,0},{4,1},{5,2},{6,3},{7,4},{8,13},{9,14},{10,... | collective-permute-start | bytes 24584 | tf_op jit(solution)/shard_map/ppermute | solution.py:15
where the time goes:
time: 290 us; the launch traced here: 284 us
  blocking collectives  141 us (49%)
  matrix products  48.6 us (17%)
  local copies, waits for them, and re-layouts  37.1 us (13%)
  other arithmetic  34 us (12%)
  waiting for transfers between devices  11.6 us (4%)
  starting transfers between devices  8.58 us (3%)
    all_gather x1, blocking collectives, on_device(): lax.all_gather(hot_taken, 'blk', axis=1, tiled=True)  51.4 us
    dot_general x32, matrix products, single(): lax.dot_general(query_part, doc_block, (((1,), (1,)), ((), ())), preferre...  48.6 us
    all_gather x1, blocking collectives, on_device(): shard_piece = lax.all_gather(published, 'blk', axis=0, tiled=True)  24.6 us
    all_gather x1, blocking collectives, on_device(): every_group = lax.all_gather(combined, 'group', axis=1, tiled=True)  23.5 us
    lt x32, other arithmetic, single(): keep_mask = jnp.arange(doc_block.shape[0], dtype=jnp.int32) < length  21.8 us
    dynamic_slice x32, local copies, waits for them, and re-layouts, maxsim(): return lax.map(single, (blocks, lengths)).T  20.7 us
    all_gather x1, blocking collectives, on_device(): lax.all_gather(candidates, 'blk', axis=1, tiled=True)  20.6 us
    all_gather x1, blocking collectives, on_device(): lax.all_gather(cand_count, 'blk', axis=1, tiled=True)  12.5 us
  transfers between devices with their start and end apart: 6, of which 2 were waited for; matrix products, arithmetic and copies ran while one was open for 41% of the time, Pallas kernels for 0%

commit v1 on v0

v1 whole, which is shorter than its diff:
```python
import functools

import jax
import jax.numpy as jnp
from jax import lax
from jax.experimental import pallas as pl
from jax.experimental.pallas import tpu as pltpu
from jax.sharding import PartitionSpec as P

TOPK = 16
MASKED_SCORE = -1e30
LANES = 128
SUB = 8


def merge_desc(seq):
    n = len(seq)
    if n == 1:
        return seq
    half = n // 2
    hi = [jnp.maximum(seq[i], seq[i + half]) for i in range(half)]
    lo = [jnp.minimum(seq[i], seq[i + half]) for i in range(half)]
    return merge_desc(hi) + merge_desc(lo)


def sort_desc(seq):
    n = len(seq)
    if n == 1:
        return seq
    return merge_desc(sort_desc(seq[: n // 2]) + sort_desc(seq[n // 2 :])[::-1])


def kernel(dims, meta_s, meta_v, q_ref, doc_ref, out_ref,
           meta_in, meta_in_s, fixed, hot, sendbuf, recv, cur, maxes, scores,
           m_send, m_recv, m_local, h_send, h_recv, d_send, d_recv, g_send, g_recv):
    shards, groups, hops, cap, per_dev, hot_pub, hot_dev, offs, at = dims
    me = lax.axis_index("blk")
    grp = lax.axis_index("group")

    def peer(o):
        return lax.rem(me + (o % shards), shards)

    def gpeer(o):
        return lax.rem(grp + o, groups)

    barrier = pltpu.get_barrier_semaphore()
    for o in range(1, shards):
        pl.semaphore_signal(barrier, inc=1, device_id={"blk": peer(o)},
                            device_id_type=pl.DeviceIdType.MESH)
    for o in range(1, groups):
        pl.semaphore_signal(barrier, inc=1, device_id={"group": gpeer(o)},
                            device_id_type=pl.DeviceIdType.MESH)

    rows, dim = doc_ref.shape[2], doc_ref.shape[3]
    row_id = lax.broadcasted_iota(jnp.int32, (rows, dim), 0)

    def fix(i, carry):
        length = meta_s[0, at["len"] + i]
        block = doc_ref[0, i].astype(jnp.float32)
        fixed[i] = jnp.where(row_id < length, block, block[0:1, :]).astype(fixed.dtype)
        return carry

    lax.fori_loop(0, per_dev, fix, 0, unroll=2)
    for m in range(hot_pub):
        hot[me * hot_pub + m] = fixed[meta_s[0, at["owned"] + m]]

    pl.semaphore_wait(barrier, shards + groups - 2)

    meta_copies = {}
    for o in offs:
        slot = offs.index((-o) % shards)
        meta_copies[o] = pltpu.make_async_remote_copy(
            src_ref=meta_v, dst_ref=meta_in.at[slot], send_sem=m_send.at[slot],
            recv_sem=m_recv.at[slot], device_id={"blk": peer(o)},
            device_id_type=pl.DeviceIdType.MESH)
        meta_copies[o].start()
    hot_copies = []
    for o in range(1, shards):
        part = hot.at[pl.ds(me * hot_pub, hot_pub)]
        c = pltpu.make_async_remote_copy(
            src_ref=part, dst_ref=part, send_sem=h_send.at[o - 1],
            recv_sem=h_recv.at[o - 1], device_id={"blk": peer(o)},
            device_id_type=pl.DeviceIdType.MESH)
        c.start()
        hot_copies.append(c)
    for o in offs:
        meta_copies[o].wait_recv()
    local = pltpu.make_async_copy(meta_in, meta_in_s, m_local)
    local.start()
    local.wait()

    doc_copies = []
    for h in range(1, hops):
        slot = offs.index((-h) % shards)
        for c in range(cap):
            want = meta_in_s[slot, 0, at["cand"] + h * cap + c]
            sendbuf[h - 1, c] = fixed[jnp.clip(want, 0, per_dev - 1)]
        d = pltpu.make_async_remote_copy(
            src_ref=sendbuf.at[h - 1], dst_ref=recv.at[h - 1], send_sem=d_send.at[h - 1],
            recv_sem=d_recv.at[h - 1], device_id={"blk": peer(-h)},
            device_id_type=pl.DeviceIdType.MESH)
        d.start()
        doc_copies.append(d)

    for c in hot_copies:
        c.wait_recv()

    segs, tiles, qtok = q_ref.shape[0], q_ref.shape[1], q_ref.shape[2]
    width = segs * qtok
    lane = lax.broadcasted_iota(jnp.int32, (cap, LANES), 1)
    cand_id = lax.broadcasted_iota(jnp.int32, (cap, width), 0)
    for h in range(hops):
        if h > 0:
            doc_copies[h - 1].wait_recv()
        for c in range(cap):
            slot_id = meta_s[0, at["cand"] + h * cap + c]
            kth = jnp.clip(slot_id - per_dev, 0, hot_dev - 1)
            if h == 0:
                entry = meta_s[0, at["taken"] + kth]
                own = fixed[jnp.clip(slot_id, 0, per_dev - 1)]
            else:
                entry = meta_in_s[offs.index(h % shards), 0, at["taken"] + kth]
                own = recv[h - 1, c]
            hot_block = hot[jnp.clip(entry, 0, shards * hot_pub - 1)]
            cur[pl.ds(c * rows, rows), :] = jnp.where(slot_id >= per_dev, hot_block, own)

        def tile_step(j, carry):
            w = q_ref[:, j].reshape(width, dim)
            s = lax.dot_general(cur[...], w, (((1,), (1,)), ((), ())),
                                preferred_element_type=jnp.float32)
            maxes[j] = jnp.max(s.reshape(cap, rows, width), axis=1)
            return carry

        lax.fori_loop(0, tiles, tile_step, 0)

        halves = []
        for half in range(width // LANES):
            acc = jnp.zeros((cap, LANES), jnp.float32)
            for j in range(tiles):
                x = maxes[j, :, half * LANES : (half + 1) * LANES]
                step = qtok // 2
                while step:
                    x = x + pltpu.roll(x, step, 1)
                    step //= 2
                x = pltpu.roll(x, (j + 1 - qtok) % LANES, 1)
                acc = jnp.where(lane % qtok == j, x, acc)
            halves.append(acc * (1.0 / qtok))
        result = jnp.concatenate(halves, axis=1)
        live = meta_s[0, at["count"] + h]
        scores[grp, pl.ds(h * cap, cap), :] = jnp.where(cand_id < live, result, MASKED_SCORE)

    g_copies = []
    for o in range(1, groups):
        c = pltpu.make_async_remote_copy(
            src_ref=scores.at[grp], dst_ref=scores.at[grp], send_sem=g_send.at[o - 1],
            recv_sem=g_recv.at[o - 1], device_id={"group": gpeer(o)},
            device_id_type=pl.DeviceIdType.MESH)
        c.start()
        g_copies.append(c)
    for c in g_copies:
        c.wait_recv()

    for half in range(width // LANES):
        cols = slice(half * LANES, (half + 1) * LANES)
        seq = [scores[g, r : r + SUB, cols] for g in range(groups)
               for r in range(0, hops * cap, SUB)]
        seq = sort_desc(seq)[:TOPK]
        shift = SUB // 2
        while shift:
            other = [pltpu.roll(v, shift, 0) for v in seq]
            n = len(seq)
            seq = merge_desc([jnp.maximum(seq[i], other[n - 1 - i]) for i in range(n)])
            shift //= 2
        out_ref[:, cols] = jnp.concatenate([v[0:1, :] for v in seq], axis=0)

    for c in list(meta_copies.values()) + hot_copies + doc_copies + g_copies:
        c.wait_send()


def on_device(shards, groups, queries, doc_blocks, doc_len, candidates, cand_count,
              hot_owned, hot_taken):
    per_dev, rows, dim = doc_blocks.shape[1:]
    hops, cap = candidates.shape[2:]
    hot_pub, hot_dev = hot_owned.shape[2], hot_taken.shape[2]
    qpb, qtok = queries.shape[0], queries.shape[1]
    fields = (("cand", candidates), ("taken", hot_taken), ("owned", hot_owned),
              ("len", doc_len), ("count", cand_count))
    at, pos = {}, 0
    for name, arr in fields:
        at[name] = pos
        pos += arr.size
    flat = jnp.concatenate([a.reshape(-1) for _, a in fields])
    meta = jnp.pad(flat, (0, SUB * LANES - pos)).reshape(SUB, LANES)
    tiles = qtok
    segs = qpb // tiles
    q4 = queries.reshape(segs, tiles, qtok, dim)
    offs = sorted({o % shards for h in range(1, hops) for o in (h, -h)})
    dims = (shards, groups, hops, cap, per_dev, hot_pub, hot_dev, offs, at)
    vmem = pl.BlockSpec(memory_space=pltpu.VMEM)
    dma = pltpu.SemaphoreType.DMA
    bf = doc_blocks.dtype
    top = pl.pallas_call(
        functools.partial(kernel, dims),
        out_shape=jax.ShapeDtypeStruct((TOPK, qpb), jnp.float32),
        in_specs=[pl.BlockSpec(memory_space=pltpu.SMEM), vmem, vmem, vmem],
        out_specs=vmem,
        scratch_shapes=[
            pltpu.VMEM((len(offs), SUB, LANES), jnp.int32),
            pltpu.SMEM((len(offs), SUB, LANES), jnp.int32),
            pltpu.VMEM((per_dev, rows, dim), bf),
            pltpu.VMEM((shards * hot_pub, rows, dim), bf),
            pltpu.VMEM((hops - 1, cap, rows, dim), bf),
            pltpu.VMEM((hops - 1, cap, rows, dim), bf),
            pltpu.VMEM((cap * rows, dim), bf),
            pltpu.VMEM((tiles, cap, segs * qtok), jnp.float32),
            pltpu.VMEM((groups, hops * cap, qpb), jnp.float32),
            dma((len(offs),)), dma((len(offs),)), dma(()),
            dma((shards - 1,)), dma((shards - 1,)),
            dma((hops - 1,)), dma((hops - 1,)),
            dma((groups - 1,)), dma((groups - 1,)),
        ],
        compiler_params=pltpu.CompilerParams(
            collective_id=0, has_side_effects=True, vmem_limit_bytes=48 * 1024 * 1024),
    )(meta, meta, q4, doc_blocks)
    return top.T


def solution(mesh):
    return jax.shard_map(
        functools.partial(on_device, mesh.shape["blk"], mesh.shape["group"]),
        mesh=mesh,
        in_specs=(
            P("blk", None, None),
            P("group", "blk", None, None),
            P("group", "blk"),
            P("group", "blk", None, None),
            P("group", "blk", None),
            P("group", "blk", None),
            P("group", "blk", None),
        ),
        out_specs=P("blk", None),
        check_vma=False,
    )
```

time: 290 us -> 81.1 us (0.28); the launches traced: 284 us -> 80.9 us
  blocking collectives: 141 us -> 0 us
  Pallas kernels: 0 us -> 75.4 us
  matrix products: 48.6 us -> 0 us
  other arithmetic: 34 us -> 0 us
  local copies, waits for them, and re-layouts: 37.1 us -> 4.77 us
  waiting for transfers between devices: 11.6 us -> 0 us
  starting transfers between devices: 8.58 us -> 0 us
    all_gather x5 -> x0, blocking collectives: 133 us -> none  [the longest x1 51.4 us: on_device(): lax.all_gather(hot_taken, 'blk', axis=1, tiled=True)]
    pallas_call x0 -> x1, Pallas kernels: none -> 75.4 us  [on_device(): pl.pallas_call(functools.partial(kernel, dims), out_shape=jax.ShapeDtypeS...]
    dot_general x32 -> x0, matrix products: 48.6 us -> none  [single(): lax.dot_general(query_part, doc_block, (((1,), (1,)), ((), ())), preferre...]
    lt x36 -> x0, other arithmetic: 24.2 us -> none  [the longest x32 21.8 us: single(): keep_mask = jnp.arange(doc_block.shape[0], dtype=jnp.int32) < length]
    dynamic_slice x33 -> x0, local copies, waits for them, and re-layouts: 21.3 us -> none  [the longest x32 20.7 us: maxsim(): return lax.map(single, (blocks, lengths)).T]
    ppermute x6 -> x0, waiting for transfers between devices: 11.6 us -> none  [shifted(): return lax.ppermute(x, axis, [(i, (i + by) % peers) for i in range(peers)])]
    ppermute x6 -> x0, starting transfers between devices: 8.58 us -> none  [shifted(): return lax.ppermute(x, axis, [(i, (i + by) % peers) for i in range(peers)])]
    squeeze x1 -> x0, blocking collectives: 8.38 us -> none  [on_device(): lengths_all[0]]
  transfers between devices with their start and end apart: 6 -> 0, of which waited for: 2 -> 0; matrix products, arithmetic and copies ran while one was open for 41% -> 0% of each run, Pallas kernels for 0% -> 0%
where the time goes in v1:
time: 81.1 us; the launch traced here: 80.9 us
  Pallas kernels  75.4 us (93%)
  local copies, waits for them, and re-layouts  4.77 us (6%)
    pallas_call x1, Pallas kernels, on_device(): pl.pallas_call(functools.partial(kernel, dims), out_shape=jax.ShapeDtypeS...  75.4 us
    unnamed x5, local copies, waits for them, and re-layouts  3.24 us

profile of v1, /device:TPU:27, one launch (start us, length us, event | category | flops | bytes accessed | tf_op | source)
XLA Modules:
  0.0 80.9 jit_solution(6472662414989381069)
XLA Ops:
  0.7 0.8 reshape.21
  1.4 0.8 concatenate.3
  2.2 0.0 copy-start
  2.2 1.6 %copy-done = bf16[256,32,128]{2,1,0:T(8,128)(2,1)S(1)} copy-done((bf16[256,32,128]{2,1,0:T(8,128)(2,1)S(1)}, bf16[256,32,128]{2,1,0:T(8,128)(2,1)}, u32[]{:S(2)}) %copy-start) | copy-done | bytes 2097176
  3.8 0.0 copy-start.1
  3.8 1.0 %copy-done.1 = bf16[1,16,128,128]{3,2,1,0:T(8,128)(2,1)S(1)} copy-done((bf16[1,16,128,128]{3,2,1,0:T(8,128)(2,1)S(1)}, bf16[1,16,128,128]{3,2,1,0:T(8,128)(2,1)}, u32[]{:S(2)}) %copy-start.1) | copy-done | bytes 524312
  4.8 75.4 %shard_map.73 = f32[16,256]{1,0:T(8,128)S(1)} custom-call(s32[8,128]{1,0:T(8,128)S(1)} %pad_bitcast_fusion.meta_s.meta_v, s32[8,128]{1,0:T(8,128)S(1)} %pad_bitcast_fusion.meta_s.meta_v, bf16[8,32,32,128]{3,2,1,0:T(8,128)(2,1)S(1)} %bitcast.9, bf16[1,16,128,128]{3,2,1,0:T(8,128)(2,1)S(1)} %copy-done.1), custom_call_target="tpu_custom_call" | custom-call | tf_op jit(solution)/shard_map/pallas_call | solution.py:202
  80.2 0.6 copy.10
  (1 shorter events, 0.0 us)
Async XLA Ops:
  2.2 1.6 %copy-start = (bf16[256,32,128]{2,1,0:T(8,128)(2,1)S(1)}, bf16[256,32,128]{2,1,0:T(8,128)(2,1)}, u32[]{:S(2)}) copy-start(bf16[256,32,128]{2,1,0:T(8,128)(2,1)} %param.7) | copy-start | bytes 6291460
  3.8 1.0 %copy-start.1 = (bf16[1,16,128,128]{3,2,1,0:T(8,128)(2,1)S(1)}, bf16[1,16,128,128]{3,2,1,0:T(8,128)(2,1)}, u32[]{:S(2)}) copy-start(bf16[1,16,128,128]{3,2,1,0:T(8,128)(2,1)} %doc_ref.1) | copy-start | bytes 1572868

commit v2 on v1

--- a/solution.py
+++ b/solution.py
@@ -10,6 +10,7 @@
 TOPK = 16
 MASKED_SCORE = -1e30
 LANES = 128
+UNROLL = 16
 SUB = 8
 
 
@@ -30,10 +31,10 @@
     return merge_desc(sort_desc(seq[: n // 2]) + sort_desc(seq[n // 2 :])[::-1])
 
 
-def kernel(dims, meta_s, meta_v, q_ref, doc_ref, out_ref,
-           meta_in, meta_in_s, fixed, hot, sendbuf, recv, cur, maxes, scores,
+def kernel(dims, len_s, cand_s, count_s, owned_s, taken_s, cand_v, taken_v, q_hbm, doc_hbm,
+           out_ref, q_ref, doc_ref, load_sem, meta_v, meta_in, meta_in_s, fixed, hot, sendbuf, recv, cur, maxes, scores,
            m_send, m_recv, m_local, h_send, h_recv, d_send, d_recv, g_send, g_recv):
-    shards, groups, hops, cap, per_dev, hot_pub, hot_dev, offs, at = dims
+    shards, groups, hops, cap, per_dev, hot_pub, hot_dev, offs = dims
     me = lax.axis_index("blk")
     grp = lax.axis_index("group")
 
@@ -51,18 +52,27 @@
         pl.semaphore_signal(barrier, inc=1, device_id={"group": gpeer(o)},
                             device_id_type=pl.DeviceIdType.MESH)
 
+    q_load = pltpu.make_async_copy(q_hbm, q_ref, load_sem.at[0])
+    doc_load = pltpu.make_async_copy(doc_hbm, doc_ref, load_sem.at[1])
+    doc_load.start()
+    q_load.start()
+    meta_v[...] = jnp.zeros_like(meta_v)
+    meta_v[0:hops, 0:cap] = cand_v[0, 0]
+    meta_v[hops : hops + 1, 0:hot_dev] = taken_v[0]
+    doc_load.wait()
+
     rows, dim = doc_ref.shape[2], doc_ref.shape[3]
     row_id = lax.broadcasted_iota(jnp.int32, (rows, dim), 0)
 
     def fix(i, carry):
-        length = meta_s[0, at["len"] + i]
+        length = len_s[0, i]
         block = doc_ref[0, i].astype(jnp.float32)
         fixed[i] = jnp.where(row_id < length, block, block[0:1, :]).astype(fixed.dtype)
         return carry
 
     lax.fori_loop(0, per_dev, fix, 0, unroll=2)
     for m in range(hot_pub):
-        hot[me * hot_pub + m] = fixed[meta_s[0, at["owned"] + m]]
+        hot[me * hot_pub + m] = fixed[owned_s[0, 0, m]]
 
     pl.semaphore_wait(barrier, shards + groups - 2)
 
@@ -93,17 +103,19 @@
     for h in range(1, hops):
         slot = offs.index((-h) % shards)
         for c in range(cap):
-            want = meta_in_s[slot, 0, at["cand"] + h * cap + c]
+            want = meta_in_s[slot, h, c]
             sendbuf[h - 1, c] = fixed[jnp.clip(want, 0, per_dev - 1)]
         d = pltpu.make_async_remote_copy(
             src_ref=sendbuf.at[h - 1], dst_ref=recv.at[h - 1], send_sem=d_send.at[h - 1],
             recv_sem=d_recv.at[h - 1], device_id={"blk": peer(-h)},
             device_id_type=pl.DeviceIdType.MESH)
-        d.start()
         doc_copies.append(d)
+        if h == 1:
+            d.start()
 
     for c in hot_copies:
         c.wait_recv()
+    q_load.wait()
 
     segs, tiles, qtok = q_ref.shape[0], q_ref.shape[1], q_ref.shape[2]
     width = segs * qtok
@@ -113,13 +125,13 @@
         if h > 0:
             doc_copies[h - 1].wait_recv()
         for c in range(cap):
-            slot_id = meta_s[0, at["cand"] + h * cap + c]
+            slot_id = cand_s[0, 0, h, c]
             kth = jnp.clip(slot_id - per_dev, 0, hot_dev - 1)
             if h == 0:
-                entry = meta_s[0, at["taken"] + kth]
+                entry = taken_s[0, 0, kth]
                 own = fixed[jnp.clip(slot_id, 0, per_dev - 1)]
             else:
-                entry = meta_in_s[offs.index(h % shards), 0, at["taken"] + kth]
+                entry = meta_in_s[offs.index(h % shards), hops, kth]
                 own = recv[h - 1, c]
             hot_block = hot[jnp.clip(entry, 0, shards * hot_pub - 1)]
             cur[pl.ds(c * rows, rows), :] = jnp.where(slot_id >= per_dev, hot_block, own)
@@ -131,7 +143,14 @@
             maxes[j] = jnp.max(s.reshape(cap, rows, width), axis=1)
             return carry
 
-        lax.fori_loop(0, tiles, tile_step, 0)
+        for part in range(2):
+            lax.fori_loop(part * tiles // 2, (part + 1) * tiles // 2, tile_step, 0,
+                          unroll=UNROLL)
+            begin = part + 2
+            if h == 0 and begin < hops:
+                doc_copies[begin - 1].start()
+        for begin in range(4, hops if h == 0 else 0):
+            doc_copies[begin - 1].start()
 
         halves = []
         for half in range(width // LANES):
@@ -146,7 +165,7 @@
                 acc = jnp.where(lane % qtok == j, x, acc)
             halves.append(acc * (1.0 / qtok))
         result = jnp.concatenate(halves, axis=1)
-        live = meta_s[0, at["count"] + h]
+        live = count_s[0, 0, h]
         scores[grp, pl.ds(h * cap, cap), :] = jnp.where(cand_id < live, result, MASKED_SCORE)
 
     g_copies = []
@@ -183,28 +202,25 @@
     hops, cap = candidates.shape[2:]
     hot_pub, hot_dev = hot_owned.shape[2], hot_taken.shape[2]
     qpb, qtok = queries.shape[0], queries.shape[1]
-    fields = (("cand", candidates), ("taken", hot_taken), ("owned", hot_owned),
-              ("len", doc_len), ("count", cand_count))
-    at, pos = {}, 0
-    for name, arr in fields:
-        at[name] = pos
-        pos += arr.size
-    flat = jnp.concatenate([a.reshape(-1) for _, a in fields])
-    meta = jnp.pad(flat, (0, SUB * LANES - pos)).reshape(SUB, LANES)
     tiles = qtok
     segs = qpb // tiles
     q4 = queries.reshape(segs, tiles, qtok, dim)
     offs = sorted({o % shards for h in range(1, hops) for o in (h, -h)})
-    dims = (shards, groups, hops, cap, per_dev, hot_pub, hot_dev, offs, at)
+    dims = (shards, groups, hops, cap, per_dev, hot_pub, hot_dev, offs)
     vmem = pl.BlockSpec(memory_space=pltpu.VMEM)
+    anym = pl.BlockSpec(memory_space=pl.ANY)
     dma = pltpu.SemaphoreType.DMA
     bf = doc_blocks.dtype
     top = pl.pallas_call(
         functools.partial(kernel, dims),
         out_shape=jax.ShapeDtypeStruct((TOPK, qpb), jnp.float32),
-        in_specs=[pl.BlockSpec(memory_space=pltpu.SMEM), vmem, vmem, vmem],
+        in_specs=[pl.BlockSpec(memory_space=pltpu.SMEM)] * 5 + [vmem] * 2 + [anym] * 2,
         out_specs=vmem,
         scratch_shapes=[
+            pltpu.VMEM(q4.shape, bf),
+            pltpu.VMEM(doc_blocks.shape, bf),
+            dma((2,)),
+            pltpu.VMEM((SUB, LANES), jnp.int32),
             pltpu.VMEM((len(offs), SUB, LANES), jnp.int32),
             pltpu.SMEM((len(offs), SUB, LANES), jnp.int32),
             pltpu.VMEM((per_dev, rows, dim), bf),
@@ -221,7 +237,8 @@
         ],
         compiler_params=pltpu.CompilerParams(
             collective_id=0, has_side_effects=True, vmem_limit_bytes=48 * 1024 * 1024),
-    )(meta, meta, q4, doc_blocks)
+    )(doc_len, candidates, cand_count, hot_owned, hot_taken, candidates, hot_taken,
+      q4, doc_blocks)
     return top.T
 
 

time: 81.1 us -> 59.5 us (0.73)
  Pallas kernels: 75.4 us -> 52.7 us
  local copies, waits for them, and re-layouts: 4.77 us -> 5.88 us
    pallas_call x1, Pallas kernels: 75.4 us -> 52.7 us  [on_device(): pl.pallas_call(functools.partial(kernel, dims), out_shape=jax.ShapeDtypeS...]
    unnamed x5 -> x13, local copies, waits for them, and re-layouts: 3.24 us -> 5.88 us
where the time goes in v2:
time: 59.5 us; the launch traced here: 59.3 us
  Pallas kernels  52.7 us (89%)
  local copies, waits for them, and re-layouts  5.88 us (10%)
  between operations  0.67 us (1%)
    pallas_call x1, Pallas kernels, on_device(): pl.pallas_call(functools.partial(kernel, dims), out_shape=jax.ShapeDtypeS...  52.7 us
    unnamed x13, local copies, waits for them, and re-layouts  5.88 us

profile of v2, /device:TPU:27, one launch (start us, length us, event | category | flops | bytes accessed | tf_op | source)
XLA Modules:
  0.0 59.3 jit_solution(7248078785810093584)
XLA Ops:
  0.7 0.0 copy-start
  0.7 1.6 %copy-done = bf16[256,32,128]{2,1,0:T(8,128)(2,1)S(1)} copy-done((bf16[256,32,128]{2,1,0:T(8,128)(2,1)S(1)}, bf16[256,32,128]{2,1,0:T(8,128)(2,1)}, u32[]{:S(2)}) %copy-start) | copy-done | bytes 2097176
  2.2 0.0 copy-start.1
  2.2 1.0 %copy-done.1 = bf16[1,16,128,128]{3,2,1,0:T(8,128)(2,1)S(1)} copy-done((bf16[1,16,128,128]{3,2,1,0:T(8,128)(2,1)S(1)}, bf16[1,16,128,128]{3,2,1,0:T(8,128)(2,1)}, u32[]{:S(2)}) %copy-start.1) | copy-done | bytes 524312
  3.3 0.0 copy-start.2
  3.3 0.7 %copy-done.2 = s32[1,1,4,8]{3,2,1,0:T(4,128)S(1)} copy-done((s32[1,1,4,8]{3,2,1,0:T(4,128)S(1)}, s32[1,1,4,8]{3,2,1,0:T(4,128)}, u32[]{:S(2)}) %copy-start.2) | copy-done | bytes 152
  4.0 0.0 copy-start.3
  4.0 0.7 %copy-done.3 = s32[1,1,2]{2,1,0:T(1,128)S(1)} copy-done((s32[1,1,2]{2,1,0:T(1,128)S(1)}, s32[1,1,2]{2,1,0:T(1,128)}, u32[]{:S(2)}) %copy-start.3) | copy-done | bytes 32
  4.6 0.0 copy-start.4
  4.6 0.7 %copy-done.4 = s32[1,16]{1,0:T(1,128)S(1)} copy-done((s32[1,16]{1,0:T(1,128)S(1)}, s32[1,16]{1,0:T(1,128)}, u32[]{:S(2)}) %copy-start.4) | copy-done | bytes 88
  5.3 0.0 copy-start.5
  5.3 0.7 %copy-done.5 = s32[1,1,4]{2,1,0:T(1,128)S(1)} copy-done((s32[1,1,4]{2,1,0:T(1,128)S(1)}, s32[1,1,4]{2,1,0:T(1,128)}, u32[]{:S(2)}) %copy-start.5) | copy-done | bytes 40
  5.9 52.7 %shard_map.73 = f32[16,256]{1,0:T(8,128)S(1)} custom-call(s32[1,16]{1,0:T(1,128)S(1)} %copy-done.4, s32[1,1,4,8]{3,2,1,0:T(4,128)S(1)} %copy-done.2, s32[1,1,4]{2,1,0:T(1,128)S(1)} %copy-done.5, s32[1,1,1]{2,1,0:T(1,128)S(6)} %copy.9.owned_s, s32[1,1,2]{2,1,0:T(1,128)S(1)} %copy-done.3, s32[1,1,4,8]{3,2,1,0:T(4,128)S(1)} %copy-done.2, ...), custom_call_target="tpu_custom_call" | custom-call | tf_op jit(solution)/shard_map/pallas_call | solution.py:214
  58.7 0.6 %copy.10 = f32[256,16]{0,1:T(8,128)} copy(f32[256,16]{0,1:T(8,128)S(1)} %bitcast.3) | data formatting | bytes 32768
Async XLA Ops:
  0.7 1.6 %copy-start = (bf16[256,32,128]{2,1,0:T(8,128)(2,1)S(1)}, bf16[256,32,128]{2,1,0:T(8,128)(2,1)}, u32[]{:S(2)}) copy-start(bf16[256,32,128]{2,1,0:T(8,128)(2,1)} %param.7) | copy-start | bytes 6291460
  2.2 1.0 %copy-start.1 = (bf16[1,16,128,128]{3,2,1,0:T(8,128)(2,1)S(1)}, bf16[1,16,128,128]{3,2,1,0:T(8,128)(2,1)}, u32[]{:S(2)}) copy-start(bf16[1,16,128,128]{3,2,1,0:T(8,128)(2,1)} %doc_hbm.1) | copy-start | bytes 1572868
  3.3 0.7 %copy-start.2 = (s32[1,1,4,8]{3,2,1,0:T(4,128)S(1)}, s32[1,1,4,8]{3,2,1,0:T(4,128)}, u32[]{:S(2)}) copy-start(s32[1,1,4,8]{3,2,1,0:T(4,128)} %cand_v.1) | copy-start | bytes 388
  4.0 0.7 %copy-start.3 = (s32[1,1,2]{2,1,0:T(1,128)S(1)}, s32[1,1,2]{2,1,0:T(1,128)}, u32[]{:S(2)}) copy-start(s32[1,1,2]{2,1,0:T(1,128)} %taken_v.1) | copy-start | bytes 28
  4.6 0.7 %copy-start.4 = (s32[1,16]{1,0:T(1,128)S(1)}, s32[1,16]{1,0:T(1,128)}, u32[]{:S(2)}) copy-start(s32[1,16]{1,0:T(1,128)} %len_s.1) | copy-start | bytes 196
  5.3 0.7 %copy-start.5 = (s32[1,1,4]{2,1,0:T(1,128)S(1)}, s32[1,1,4]{2,1,0:T(1,128)}, u32[]{:S(2)}) copy-start(s32[1,1,4]{2,1,0:T(1,128)} %count_s.1) | copy-start | bytes 52

commit v3 on v2

--- a/solution.py
+++ b/solution.py
@@ -10,7 +10,6 @@
 TOPK = 16
 MASKED_SCORE = -1e30
 LANES = 128
-UNROLL = 16
 SUB = 8
 
 
@@ -33,7 +32,8 @@
 
 def kernel(dims, len_s, cand_s, count_s, owned_s, taken_s, cand_v, taken_v, q_hbm, doc_hbm,
            out_ref, q_ref, doc_ref, load_sem, meta_v, meta_in, meta_in_s, fixed, hot, sendbuf, recv, cur, maxes, scores,
-           m_send, m_recv, m_local, h_send, h_recv, d_send, d_recv, g_send, g_recv):
+           m_send, m_recv, m_local, h_send, h_recv, d_send, d_recv, g_send, g_recv,
+           r_send, r_recv, relay):
     shards, groups, hops, cap, per_dev, hot_pub, hot_dev, offs = dims
     me = lax.axis_index("blk")
     grp = lax.axis_index("group")
@@ -110,8 +110,32 @@
             recv_sem=d_recv.at[h - 1], device_id={"blk": peer(-h)},
             device_id_type=pl.DeviceIdType.MESH)
         doc_copies.append(d)
-        if h == 1:
-            d.start()
+    far = hops - 1
+    relayed = far % 2 == 1 and far > 1 and shards % 2 == 0 and cap % 2 == 0
+    part_a = pl.ds(0, cap // 2)
+    part_b = pl.ds(cap // 2, cap // 2)
+    even = lax.rem(me, 2) == 0
+    if relayed:
+        def piece(src, dst, i, to):
+            return pltpu.make_async_remote_copy(
+                src_ref=src, dst_ref=dst, send_sem=r_send.at[i], recv_sem=r_recv.at[i],
+                device_id={"blk": peer(to)}, device_id_type=pl.DeviceIdType.MESH)
+
+        doc_copies[far - 1] = piece(sendbuf.at[far - 1, part_a], recv.at[far - 1, part_a], 0, -far)
+        straight = piece(sendbuf.at[far - 1, part_b], recv.at[far - 1, part_b], 1, -far)
+        first_leg = piece(sendbuf.at[far - 1, part_b], relay, 2, -far - 1)
+        last_leg = piece(relay, recv.at[far - 1, part_b], 1, 1)
+
+        @pl.when(even)
+        def _():
+            first_leg.start()
+
+        @pl.when(jnp.logical_not(even))
+        def _():
+            straight.start()
+
+    for d in doc_copies:
+        d.start()
 
     for c in hot_copies:
         c.wait_recv()
@@ -124,6 +148,8 @@
     for h in range(hops):
         if h > 0:
             doc_copies[h - 1].wait_recv()
+            if relayed and h == far:
+                straight.wait_recv()
         for c in range(cap):
             slot_id = cand_s[0, 0, h, c]
             kth = jnp.clip(slot_id - per_dev, 0, hot_dev - 1)
@@ -143,14 +169,15 @@
             maxes[j] = jnp.max(s.reshape(cap, rows, width), axis=1)
             return carry
 
-        for part in range(2):
-            lax.fori_loop(part * tiles // 2, (part + 1) * tiles // 2, tile_step, 0,
-                          unroll=UNROLL)
-            begin = part + 2
-            if h == 0 and begin < hops:
-                doc_copies[begin - 1].start()
-        for begin in range(4, hops if h == 0 else 0):
-            doc_copies[begin - 1].start()
+        parts = 2 if h == 0 else 1
+        for part in range(parts):
+            lax.fori_loop(part * tiles // parts, (part + 1) * tiles // parts, tile_step, 0,
+                          unroll=tiles // parts)
+        if h == 0 and relayed:
+            @pl.when(even)
+            def _():
+                first_leg.wait_recv()
+                last_leg.start()
 
         halves = []
         for half in range(width // LANES):
@@ -191,6 +218,13 @@
             seq = merge_desc([jnp.maximum(seq[i], other[n - 1 - i]) for i in range(n)])
             shift //= 2
         out_ref[:, cols] = jnp.concatenate([v[0:1, :] for v in seq], axis=0)
+
+    if relayed:
+        straight.wait_send()
+
+        @pl.when(even)
+        def _():
+            first_leg.wait_send()
 
     for c in list(meta_copies.values()) + hot_copies + doc_copies + g_copies:
         c.wait_send()
@@ -234,6 +268,8 @@
             dma((shards - 1,)), dma((shards - 1,)),
             dma((hops - 1,)), dma((hops - 1,)),
             dma((groups - 1,)), dma((groups - 1,)),
+            dma((3,)), dma((3,)),
+            pltpu.VMEM((cap // 2, rows, dim), bf),
         ],
         compiler_params=pltpu.CompilerParams(
             collective_id=0, has_side_effects=True, vmem_limit_bytes=48 * 1024 * 1024),

time: 59.5 us -> 60 us (level)
  no operation moved by 1% of the time
where the time goes in v3:
time: 60 us; the launch traced here: 59.8 us
  Pallas kernels  53.2 us (89%)
  local copies, waits for them, and re-layouts  5.88 us (10%)
  between operations  0.67 us (1%)
    pallas_call x1, Pallas kernels, on_device(): pl.pallas_call(functools.partial(kernel, dims), out_shape=jax.ShapeDtypeS...  53.2 us
    unnamed x13, local copies, waits for them, and re-layouts  5.88 us

profile of v3, /device:TPU:27, one launch (start us, length us, event | category | flops | bytes accessed | tf_op | source)
XLA Modules:
  0.0 59.8 jit_solution(2230262044679155949)
XLA Ops:
  0.7 0.0 copy-start
  0.7 1.6 %copy-done = bf16[256,32,128]{2,1,0:T(8,128)(2,1)S(1)} copy-done((bf16[256,32,128]{2,1,0:T(8,128)(2,1)S(1)}, bf16[256,32,128]{2,1,0:T(8,128)(2,1)}, u32[]{:S(2)}) %copy-start) | copy-done | bytes 2097176
  2.2 0.0 copy-start.1
  2.2 1.0 %copy-done.1 = bf16[1,16,128,128]{3,2,1,0:T(8,128)(2,1)S(1)} copy-done((bf16[1,16,128,128]{3,2,1,0:T(8,128)(2,1)S(1)}, bf16[1,16,128,128]{3,2,1,0:T(8,128)(2,1)}, u32[]{:S(2)}) %copy-start.1) | copy-done | bytes 524312
  3.3 0.0 copy-start.2
  3.3 0.7 %copy-done.2 = s32[1,1,4,8]{3,2,1,0:T(4,128)S(1)} copy-done((s32[1,1,4,8]{3,2,1,0:T(4,128)S(1)}, s32[1,1,4,8]{3,2,1,0:T(4,128)}, u32[]{:S(2)}) %copy-start.2) | copy-done | bytes 152
  4.0 0.0 copy-start.3
  4.0 0.7 %copy-done.3 = s32[1,1,2]{2,1,0:T(1,128)S(1)} copy-done((s32[1,1,2]{2,1,0:T(1,128)S(1)}, s32[1,1,2]{2,1,0:T(1,128)}, u32[]{:S(2)}) %copy-start.3) | copy-done | bytes 32
  4.6 0.0 copy-start.4
  4.6 0.7 %copy-done.4 = s32[1,16]{1,0:T(1,128)S(1)} copy-done((s32[1,16]{1,0:T(1,128)S(1)}, s32[1,16]{1,0:T(1,128)}, u32[]{:S(2)}) %copy-start.4) | copy-done | bytes 88
  5.3 0.0 copy-start.5
  5.3 0.7 %copy-done.5 = s32[1,1,4]{2,1,0:T(1,128)S(1)} copy-done((s32[1,1,4]{2,1,0:T(1,128)S(1)}, s32[1,1,4]{2,1,0:T(1,128)}, u32[]{:S(2)}) %copy-start.5) | copy-done | bytes 40
  5.9 53.2 %shard_map.73 = f32[16,256]{1,0:T(8,128)S(1)} custom-call(s32[1,16]{1,0:T(1,128)S(1)} %copy-done.4, s32[1,1,4,8]{3,2,1,0:T(4,128)S(1)} %copy-done.2, s32[1,1,4]{2,1,0:T(1,128)S(1)} %copy-done.5, s32[1,1,1]{2,1,0:T(1,128)S(6)} %copy.9.owned_s, s32[1,1,2]{2,1,0:T(1,128)S(1)} %copy-done.3, s32[1,1,4,8]{3,2,1,0:T(4,128)S(1)} %copy-done.2, ...), custom_call_target="tpu_custom_call" | custom-call | tf_op jit(solution)/shard_map/pallas_call | solution.py:248
  59.2 0.6 %copy.10 = f32[256,16]{0,1:T(8,128)} copy(f32[256,16]{0,1:T(8,128)S(1)} %bitcast.3) | data formatting | bytes 32768
Async XLA Ops:
  0.7 1.6 %copy-start = (bf16[256,32,128]{2,1,0:T(8,128)(2,1)S(1)}, bf16[256,32,128]{2,1,0:T(8,128)(2,1)}, u32[]{:S(2)}) copy-start(bf16[256,32,128]{2,1,0:T(8,128)(2,1)} %param.7) | copy-start | bytes 6291460
  2.2 1.0 %copy-start.1 = (bf16[1,16,128,128]{3,2,1,0:T(8,128)(2,1)S(1)}, bf16[1,16,128,128]{3,2,1,0:T(8,128)(2,1)}, u32[]{:S(2)}) copy-start(bf16[1,16,128,128]{3,2,1,0:T(8,128)(2,1)} %doc_hbm.1) | copy-start | bytes 1572868
  3.3 0.7 %copy-start.2 = (s32[1,1,4,8]{3,2,1,0:T(4,128)S(1)}, s32[1,1,4,8]{3,2,1,0:T(4,128)}, u32[]{:S(2)}) copy-start(s32[1,1,4,8]{3,2,1,0:T(4,128)} %cand_v.1) | copy-start | bytes 388
  4.0 0.7 %copy-start.3 = (s32[1,1,2]{2,1,0:T(1,128)S(1)}, s32[1,1,2]{2,1,0:T(1,128)}, u32[]{:S(2)}) copy-start(s32[1,1,2]{2,1,0:T(1,128)} %taken_v.1) | copy-start | bytes 28
  4.6 0.7 %copy-start.4 = (s32[1,16]{1,0:T(1,128)S(1)}, s32[1,16]{1,0:T(1,128)}, u32[]{:S(2)}) copy-start(s32[1,16]{1,0:T(1,128)} %len_s.1) | copy-start | bytes 196
  5.3 0.7 %copy-start.5 = (s32[1,1,4]{2,1,0:T(1,128)S(1)}, s32[1,1,4]{2,1,0:T(1,128)}, u32[]{:S(2)}) copy-start(s32[1,1,4]{2,1,0:T(1,128)} %count_s.1) | copy-start | bytes 52
